TPU v7x, 32 devices: a whole 2x2x4 slice. The times are simulated.
32 devices in a mesh: orbit: 2 (over y), lon: 4 (over z), lat: 4 (over x, core).
Axes of the slice: x: 2, y: 2, z: 4, core: 2. Of those that a mesh axis runs over, the one named last changes fastest.
Arguments:
- kernel: float32 [20, 131072], P(None, ('orbit', 'lon', 'lat')), may hold values from 0.2 to 1.2
- residual: float32 [131072], P(('orbit', 'lon', 'lat')), may hold values from -6 to 6
- owner_block: int32 [131072, 1], P(('orbit', 'lon', 'lat')), may hold values from 0 to 15; in each aligned block of 4096 rows (0 to 4095, 4096 to 8191, ...) at most 1024 rows name the same one
- column: int32 [131072], P(('orbit', 'lon', 'lat')), may hold values from 0 to 1023
- time_step: int32 [131072], P(('orbit', 'lon', 'lat')), may hold values from 0 to 7
- horizontal: float32 [4, 72, 32, 512], P(None, None, 'lon', 'lat'), may hold values from 0.04 to 0.22
- vertical: float32 [71, 32, 512], P(None, 'lon', 'lat'), may hold values from 0.02 to 0.24
Outputs:
- adjoint_state: float32 [72, 32, 512], P(None, 'lon', 'lat')
- flux_gradient: float32 [32, 512], P('lon', 'lat')
Inputs may be any that keep to these rules, and one draw needn't show every extreme that they name: `owner_block`: among the soundings of one device no block is named more than 1024 times, and in some device's soundings one block is named exactly 1024 times.
All inputs are finite; a program needn't handle non-finite values.
Results may differ from a plain program's by a relative error of at most 0.0001.
Values sent between devices are 32-bit elements; how exact they have to be, the bound alone decides.
A program may use at most 128 MiB of HBM per device.

v0:
```python
import jax
import jax.numpy as jnp
from jax import lax
from jax.sharding import PartitionSpec as P

LEV = 72
KLEV = 20
STEPS = 8
CLON = 8
CLAT = 128


def padded(block, sides, width, periodic):
    for axis, dim in sides:
        count = lax.axis_size(axis)
        forward = [(i, i + 1) for i in range(count - 1)]
        if periodic:
            forward.append((count - 1, 0))
        backward = [(target, source) for source, target in forward]
        low = lax.ppermute(
            lax.slice_in_dim(block, block.shape[dim] - width, None, axis=dim), axis, forward
        )
        high = lax.ppermute(lax.slice_in_dim(block, 0, width, axis=dim), axis, backward)
        block = jnp.concatenate([low, block, high], axis=dim)
    return block


def level_map(levels, kernel_levels):
    heights = jnp.arange(levels, dtype=jnp.float32)
    centre = jnp.clip((heights + 0.5) * kernel_levels / levels - 0.5, 0.0, kernel_levels - 1.0)
    knots = jnp.arange(kernel_levels, dtype=jnp.float32)
    return jnp.maximum(0.0, 1.0 - jnp.abs(centre[:, None] - knots[None, :]))


def build_slots(kernel, residual, owner_block, column, time_step, owners, capacity, cells):
    owner_ids = owner_block[:, 0]
    total_rows = owner_ids.shape[0]
    ordering = jnp.argsort(owner_ids, stable=True)
    sorted_owner = owner_ids[ordering]
    labels = jnp.arange(owners, dtype=jnp.int32)
    matches = (owner_ids[:, None] == labels[None, :]).astype(jnp.int32)
    counts = jnp.sum(matches, axis=0)
    starts = jnp.cumsum(counts) - counts
    first_slot = jnp.sum(
        jnp.where(sorted_owner[:, None] == labels[None, :], starts[None, :], 0), axis=1
    )
    slot_place = sorted_owner * capacity + jnp.arange(total_rows, dtype=jnp.int32) - first_slot
    weighted = kernel * residual[None, :]
    slot_values = (
        jnp.zeros((kernel.shape[0], owners * capacity), jnp.float32)
        .at[:, slot_place]
        .set(weighted[:, ordering])
    )
    segment = time_step * cells + column
    slot_segment = jnp.zeros((owners * capacity,), jnp.int32).at[slot_place].set(segment[ordering])
    return (slot_values, slot_segment)


def per_device(kernel, residual, owner_block, column, time_step, horizontal, vertical):
    lon_count = lax.axis_size("lon")
    lat_count = lax.axis_size("lat")
    owners = lon_count * lat_count
    capacity = 4 * kernel.shape[1] // owners
    cells = CLON * CLAT
    slot_values, slot_segment = build_slots(
        kernel, residual, owner_block, column, time_step, owners, capacity, cells
    )
    send_values = slot_values.reshape(KLEV, owners, capacity)
    send_segment = slot_segment.reshape(1, owners, capacity)
    got_values, got_segment = (
        lax.all_to_all(send_values, ("lon", "lat"), split_axis=1, concat_axis=1, tiled=True),
        lax.all_to_all(send_segment, ("lon", "lat"), split_axis=1, concat_axis=1, tiled=True),
    )
    got_values = got_values.reshape(KLEV, owners * capacity)
    got_segment = got_segment.reshape(owners * capacity)
    local_bins = jnp.zeros((KLEV, STEPS * cells), jnp.float32).at[:, got_segment].add(got_values)
    binned = lax.psum(local_bins, "orbit")
    binned = binned.reshape(KLEV, STEPS, cells)
    interp = level_map(LEV, KLEV)
    diagonal_part = 1.0 - horizontal[0] - horizontal[1] - horizontal[2] - horizontal[3]
    adjoint = jnp.zeros((LEV, CLON, CLAT), jnp.float32)
    flux_total = jnp.zeros((CLON, CLAT), jnp.float32)
    for step_index in range(STEPS - 1, -1, -1):
        forcing = jnp.dot(interp, binned[:, step_index, :], precision=lax.Precision.HIGHEST)
        forced = adjoint + forcing.reshape(LEV, CLON, CLAT)
        up_flux = vertical * (forced[1:] - forced[:-1])
        mixed = (
            forced
            + jnp.pad(up_flux, ((0, 1), (0, 0), (0, 0)))
            - jnp.pad(up_flux, ((1, 0), (0, 0), (0, 0)))
        )
        terms = horizontal * mixed[None]
        lon_edges = jnp.stack([terms[1][:, 0, :], terms[0][:, -1, :]]).reshape(2, LEV * CLAT)
        lon_padded = padded(lon_edges, (("lon", 0),), 1, True)
        lat_edges = jnp.stack([terms[3][:, :, 0], terms[2][:, :, -1]]).reshape(2, LEV * CLON)
        lat_padded = padded(lat_edges, (("lat", 0),), 1, False)
        from_west = lon_padded[0].reshape(LEV, 1, CLAT)
        from_east = lon_padded[3].reshape(LEV, 1, CLAT)
        from_south = lat_padded[0].reshape(LEV, CLON, 1)
        from_north = lat_padded[3].reshape(LEV, CLON, 1)
        east_term = jnp.concatenate([from_west, terms[0][:, :-1, :]], axis=1)
        west_term = jnp.concatenate([terms[1][:, 1:, :], from_east], axis=1)
        north_term = jnp.concatenate([from_south, terms[2][:, :, :-1]], axis=2)
        south_term = jnp.concatenate([terms[3][:, :, 1:], from_north], axis=2)
        adjoint = diagonal_part * mixed + east_term + west_term + north_term + south_term
        flux_total = flux_total + adjoint[0]
    return (adjoint, flux_total)


def solution(mesh):
    placed = (
        P(None, ("orbit", "lon", "lat")),
        P(("orbit", "lon", "lat")),
        P(("orbit", "lon", "lat"), None),
        P(("orbit", "lon", "lat")),
        P(("orbit", "lon", "lat")),
        P(None, None, "lon", "lat"),
        P(None, "lon", "lat"),
    )
    return jax.shard_map(
        per_device,
        mesh=mesh,
        in_specs=placed,
        out_specs=(P(None, "lon", "lat"), P("lon", "lat")),
        check_vma=False,
    )
```

profile of v0, /device:TPU:0, one launch (start us, length us, event | category | flops | bytes accessed | tf_op | source)
XLA Modules:
  0.0 498.3 jit_solution(1058211512279651864)
XLA Ops:
  8.1 6.5 %sort.17 = (s32[4096]{0:T(1024)}, s32[4096]{0:T(1024)S(1)}) sort(s32[4096]{0:T(1024)} %bitcast.267, s32[4096]{0:T(1024)S(1)} %iota.36), dimensions={0}, to_apply=%region_0.0 | sort | flops 49152 | bytes 65536 | tf_op jit(solution)/shard_map/jit(argsort)/sort | solution.py:38
  15.4 23.0 %gather_fusion = s32[4096]{0:T(1024)S(1)} fusion(s32[4096]{0:T(1024)S(1)} %bitcast.268, s32[4096]{0:T(1024)S(1)} %get-tuple-element.68), kind=kCustom, calls=%fused_computation | custom fusion | bytes 49152 | tf_op jit(solution)/shard_map/gather | solution.py:39
  38.8 23.0 %gather_fusion.1 = s32[4096]{0:T(1024)S(1)} fusion(s32[4096]{0:T(1024)S(1)} %get-tuple-element.69, s32[4096]{0:T(1024)S(1)} %get-tuple-element.68), kind=kCustom, calls=%fused_computation.1 | custom fusion | bytes 49152 | tf_op jit(solution)/shard_map/gather | solution.py:55
  61.9 16.1 %scatter_custom_fusion = s32[16384]{0:T(1024)} fusion(s32[4096]{0:T(1024)S(1)} %bitcast.312, s32[4096]{0:T(1024)S(1)} %gather_fusion.1, s32[]{:T(128)} %constant.17.clone.1), kind=kCustom, calls=%fused_computation.187 | custom fusion | bytes 65540 | tf_op jit(solution)/shard_map/scatter | solution.py:55
  78.0 7.4 %all-to-all-start = ((s32[1,16,1024]{2,0,1:T(1,128)}), s32[1,16,1024]{2,0,1:T(1,128)S(1)}, u32[]{:S(2)}, u32[]{:S(2)}) async-start(s32[1,16,1024]{2,0,1:T(1,128)} %bitcast.6), calls=%async_computation | async-start | bytes 131072 | tf_op jit(solution)/shard_map/all_to_all | solution.py:72
  85.4 2.0 copy.302
  87.5 37.3 %scatter_custom_fusion.1 = f32[20,16384]{0,1:T(8,128)} fusion(s32[4096]{0:T(1024)S(1)} %bitcast.313, f32[]{:T(128)} %constant.12.clone.1, f32[20,4096]{0,1:T(8,128)} %copy.302, s32[4096]{0:T(1024)S(1)} %get-tuple-element.68), kind=kCustom, calls=%fused_computation.6 | custom fusion | bytes 1311232 | tf_op jit(solution)/shard_map/scatter | solution.py:52
  124.7 6.2 %copy.303 = f32[20,16,1024]{2,0,1:T(8,128)} copy(f32[20,16,1024]{0,2,1:T(8,128)} %bitcast.269) | data formatting | bytes 2621440 | tf_op jit(solution)/shard_map/reshape | solution.py:68
  131.0 6.0 %all-to-all-start.1 = ((f32[20,16,1024]{2,0,1:T(8,128)}), f32[20,16,1024]{2,0,1:T(8,128)S(1)}, u32[]{:S(2)}, u32[]{:S(2)}) async-start(f32[20,16,1024]{2,0,1:T(8,128)} %copy.303), calls=%async_computation.1 | async-start | bytes 3145728 | tf_op jit(solution)/shard_map/all_to_all | solution.py:71
  137.3 31.7 %all-to-all-done.1 = f32[20,16,1024]{2,0,1:T(8,128)S(1)} async-done(((f32[20,16,1024]{2,0,1:T(8,128)}), f32[20,16,1024]{2,0,1:T(8,128)S(1)}, u32[]{:S(2)}, u32[]{:S(2)}) %all-to-all-start.1) | async-done | bytes 1310752 | tf_op jit(solution)/shard_map/all_to_all | solution.py:71
  170.8 4.7 copy.305
  175.5 111.6 %scatter_custom_fusion.2 = f32[20,8192]{0,1:T(8,128)} fusion(s32[16384]{0:T(1024)S(1)} %bitcast.309, f32[16384,20]{1,0:T(8,128)} %copy.305, f32[]{:T(128)} %constant.12.clone.1), kind=kCustom, calls=%fused_computation.9 | custom fusion | flops 327680 | bytes 655872 | tf_op jit(solution)/shard_map/scatter-add | solution.py:76
  287.1 3.6 copy.306
  290.8 40.5 %all-reduce.18.cloned.1.call-done = f32[20,8,1024]{2,0,1:T(8,128)} async-done(((f32[20,8,1024]{2,0,1:T(8,128)}), f32[20,8,1024]{2,0,1:T(8,128)}) %all-reduce.18.cloned.1.call-update) | async-done | bytes 655376 | tf_op jit(solution)/shard_map/psum | solution.py:77
  334.5 1.7 collective-permute-start.2
  338.4 1.5 collective-permute-start
  340.6 2.3 collective-permute-start.1
  342.9 1.9 fusion.110
  352.4 2.3 copy_add_fusion.6
  356.6 3.7 collective-permute-start.6
  364.6 3.8 collective-permute-start.5
  368.4 1.5 slice_bitcast_fusion.36
  372.7 2.2 copy_add_fusion.5
  376.9 4.3 collective-permute-start.10
  385.4 3.8 collective-permute-start.9
  389.2 2.1 fusion.42
  391.3 1.5 copy.345
  395.6 2.2 copy_add_fusion.4
  399.9 4.3 collective-permute-start.14
  408.3 3.8 collective-permute-start.13
  412.2 1.5 slice_bitcast_fusion.35
  416.5 2.1 copy_add_fusion.3
  419.2 4.3 collective-permute-start.18
  426.3 3.8 collective-permute-start.17
  430.2 2.1 fusion.40
  432.2 1.5 copy.346
  436.6 2.1 copy_add_fusion.2
  439.4 4.3 collective-permute-start.22
  447.9 3.8 collective-permute-start.21
  451.7 1.5 slice_bitcast_fusion.34
  456.1 2.1 copy_add_fusion.1
  458.8 4.3 collective-permute-start.26
  465.9 3.8 collective-permute-start.25
  474.0 2.1 copy_add_fusion
  476.7 4.3 collective-permute-start.30
  481.1 3.9 collective-permute-start.29
  487.0 2.6 collective-permute-done.31
  490.1 1.4 fusion.86
  (242 shorter events, 69.2 us)
Async XLA Ops:
  7.2 8.2 %copy-start = (s32[4096,1]{0,1:T(1,128)S(1)}, s32[4096,1]{0,1:T(1,128)}, u32[]{:S(2)}) copy-start(s32[4096,1]{0,1:T(1,128)} %param.9) | copy-start | bytes 49156
  38.8 46.6 %copy-start.12 = (f32[20,4096]{1,0:T(8,128)S(1)}, f32[20,4096]{1,0:T(8,128)}, u32[]{:S(2)}) copy-start(f32[20,4096]{1,0:T(8,128)} %param.7) | copy-start | bytes 983044
  38.8 46.6 %copy-start.14 = (f32[4096]{0:T(1024)S(1)}, f32[4096]{0:T(1024)}, u32[]{:S(2)}) copy-start(f32[4096]{0:T(1024)} %param.8) | copy-start | bytes 49156
  78.0 53.0 %all-to-all-start = ((s32[1,16,1024]{2,0,1:T(1,128)}), s32[1,16,1024]{2,0,1:T(1,128)S(1)}, u32[]{:S(2)}, u32[]{:S(2)}) async-start(s32[1,16,1024]{2,0,1:T(1,128)} %bitcast.6), calls=%async_computation | async-start | bytes 131072 | tf_op jit(solution)/shard_map/all_to_all | solution.py:72
  131.0 38.0 %all-to-all-start.1 = ((f32[20,16,1024]{2,0,1:T(8,128)}), f32[20,16,1024]{2,0,1:T(8,128)S(1)}, u32[]{:S(2)}, u32[]{:S(2)}) async-start(f32[20,16,1024]{2,0,1:T(8,128)} %copy.303), calls=%async_computation.1 | async-start | bytes 3145728 | tf_op jit(solution)/shard_map/all_to_all | solution.py:71
  137.0 194.3 %all-reduce.18.cloned.1.call-start = ((), (), s32[]{:S(2)}) async-start(), calls=%async_computation.2 | async-start | bytes 1572864 | tf_op jit(solution)/shard_map/psum | solution.py:77
  290.7 42.1 %copy-start.2 = (f32[71,8,128]{2,1,0:T(8,128)S(1)}, f32[71,8,128]{2,1,0:T(8,128)}, u32[]{:S(2)}) copy-start(f32[71,8,128]{2,1,0:T(8,128)} %param.13) | copy-start | bytes 872452
  334.5 15.9 %collective-permute-start.2 = (f32[1,576]{1,0:T(1,128)S(1)}, f32[1,576]{1,0:T(1,128)S(1)}, u32[]{:S(2)}, u32[]{:S(2)}) collective-permute-start(f32[1,576]{1,0:T(1,128)S(1)} %slice.575), channel_id=1, source_target_pairs={{0,1},{1,2},{2,3},{4,5},{5,6},{6,7},{8,9},{9,10},{10,11},{12,13},{... | collective-permute-start | bytes 6920 | tf_op jit(solution)/shard_map/ppermute | solution.py:20
  336.5 14.9 %collective-permute-start.3 = (f32[1,576]{1,0:T(1,128)S(1)}, f32[1,576]{1,0:T(1,128)S(1)}, u32[]{:S(2)}, u32[]{:S(2)}) collective-permute-start(f32[1,576]{1,0:T(1,128)S(1)} %slice.580), channel_id=1, source_target_pairs={{1,0},{2,1},{3,2},{5,4},{6,5},{7,6},{9,8},{10,9},{11,10},{13,12},{... | collective-permute-start | bytes 6920 | tf_op jit(solution)/shard_map/ppermute | solution.py:23
  338.4 13.9 %collective-permute-start = (f32[1,9216]{1,0:T(1,128)}, f32[1,9216]{1,0:T(1,128)}, u32[]{:S(2)}, u32[]{:S(2)}) collective-permute-start(f32[1,9216]{1,0:T(1,128)} %slice_bitcast_fusion.56), channel_id=1, source_target_pairs={{0,4},{4,8},{8,12},{12,0},{1,5},{5,9},{9,13},{13,1},{2,6},{6,10},{... | collective-permute-start | bytes 110600 | tf_op jit(solution)/shard_map/ppermute | solution.py:20
  340.6 11.8 %collective-permute-start.1 = (f32[1,9216]{1,0:T(1,128)}, f32[1,9216]{1,0:T(1,128)}, u32[]{:S(2)}, u32[]{:S(2)}) collective-permute-start(f32[1,9216]{1,0:T(1,128)} %slice_bitcast_fusion.55), channel_id=1, source_target_pairs={{4,0},{8,4},{12,8},{0,12},{5,1},{9,5},{13,9},{1,13},{6,2},{10,6},{... | collective-permute-start | bytes 110600 | tf_op jit(solution)/shard_map/ppermute | solution.py:23
  348.9 3.4 copy-start.6
  356.6 14.9 %collective-permute-start.6 = (f32[1,576]{1,0:T(1,128)S(1)}, f32[1,576]{1,0:T(1,128)S(1)}, u32[]{:S(2)}, u32[]{:S(2)}) collective-permute-start(f32[1,576]{1,0:T(1,128)S(1)} %slice.594), channel_id=1, source_target_pairs={{0,1},{1,2},{2,3},{4,5},{5,6},{6,7},{8,9},{9,10},{10,11},{12,13},{... | collective-permute-start | bytes 6920 | tf_op jit(solution)/shard_map/ppermute | solution.py:20
  362.0 9.8 %collective-permute-start.7 = (f32[1,576]{1,0:T(1,128)S(1)}, f32[1,576]{1,0:T(1,128)S(1)}, u32[]{:S(2)}, u32[]{:S(2)}) collective-permute-start(f32[1,576]{1,0:T(1,128)S(1)} %slice.599), channel_id=1, source_target_pairs={{1,0},{2,1},{3,2},{5,4},{6,5},{7,6},{9,8},{10,9},{11,10},{13,12},{... | collective-permute-start | bytes 6920 | tf_op jit(solution)/shard_map/ppermute | solution.py:23
  363.9 8.8 %collective-permute-start.4 = (f32[1,9216]{1,0:T(1,128)}, f32[1,9216]{1,0:T(1,128)}, u32[]{:S(2)}, u32[]{:S(2)}) collective-permute-start(f32[1,9216]{1,0:T(1,128)} %slice_bitcast_fusion.54), channel_id=1, source_target_pairs={{0,4},{4,8},{8,12},{12,0},{1,5},{5,9},{9,13},{13,1},{2,6},{6,10},{... | collective-permute-start | bytes 110600 | tf_op jit(solution)/shard_map/ppermute | solution.py:20
  364.6 8.1 %collective-permute-start.5 = (f32[1,9216]{1,0:T(1,128)}, f32[1,9216]{1,0:T(1,128)}, u32[]{:S(2)}, u32[]{:S(2)}) collective-permute-start(f32[1,9216]{1,0:T(1,128)} %slice_bitcast_fusion.53), channel_id=1, source_target_pairs={{4,0},{8,4},{12,8},{0,12},{5,1},{9,5},{13,9},{1,13},{6,2},{10,6},{... | collective-permute-start | bytes 110600 | tf_op jit(solution)/shard_map/ppermute | solution.py:23
  370.6 2.1 copy-start.4
  376.9 17.5 %collective-permute-start.10 = (f32[1,576]{1,0:T(1,128)S(1)}, f32[1,576]{1,0:T(1,128)S(1)}, u32[]{:S(2)}, u32[]{:S(2)}) collective-permute-start(f32[1,576]{1,0:T(1,128)S(1)} %slice.613), channel_id=1, source_target_pairs={{0,1},{1,2},{2,3},{4,5},{5,6},{6,7},{8,9},{9,10},{10,11},{12,13},{... | collective-permute-start | bytes 6920 | tf_op jit(solution)/shard_map/ppermute | solution.py:20
  382.8 11.8 %collective-permute-start.11 = (f32[1,576]{1,0:T(1,128)S(1)}, f32[1,576]{1,0:T(1,128)S(1)}, u32[]{:S(2)}, u32[]{:S(2)}) collective-permute-start(f32[1,576]{1,0:T(1,128)S(1)} %slice.618), channel_id=1, source_target_pairs={{1,0},{2,1},{3,2},{5,4},{6,5},{7,6},{9,8},{10,9},{11,10},{13,12},{... | collective-permute-start | bytes 6920 | tf_op jit(solution)/shard_map/ppermute | solution.py:23
  384.7 10.9 %collective-permute-start.8 = (f32[1,9216]{1,0:T(1,128)}, f32[1,9216]{1,0:T(1,128)}, u32[]{:S(2)}, u32[]{:S(2)}) collective-permute-start(f32[1,9216]{1,0:T(1,128)} %slice_bitcast_fusion.52), channel_id=1, source_target_pairs={{0,4},{4,8},{8,12},{12,0},{1,5},{5,9},{9,13},{13,1},{2,6},{6,10},{... | collective-permute-start | bytes 110600 | tf_op jit(solution)/shard_map/ppermute | solution.py:20
  385.4 10.2 %collective-permute-start.9 = (f32[1,9216]{1,0:T(1,128)}, f32[1,9216]{1,0:T(1,128)}, u32[]{:S(2)}, u32[]{:S(2)}) collective-permute-start(f32[1,9216]{1,0:T(1,128)} %slice_bitcast_fusion.51), channel_id=1, source_target_pairs={{4,0},{8,4},{12,8},{0,12},{5,1},{9,5},{13,9},{1,13},{6,2},{10,6},{... | collective-permute-start | bytes 110600 | tf_op jit(solution)/shard_map/ppermute | solution.py:23
  393.5 2.1 copy-start.7
  399.9 15.4 %collective-permute-start.14 = (f32[1,576]{1,0:T(1,128)S(1)}, f32[1,576]{1,0:T(1,128)S(1)}, u32[]{:S(2)}, u32[]{:S(2)}) collective-permute-start(f32[1,576]{1,0:T(1,128)S(1)} %slice.632), channel_id=1, source_target_pairs={{0,1},{1,2},{2,3},{4,5},{5,6},{6,7},{8,9},{9,10},{10,11},{12,13},{... | collective-permute-start | bytes 6920 | tf_op jit(solution)/shard_map/ppermute | solution.py:20
  405.7 9.8 %collective-permute-start.15 = (f32[1,576]{1,0:T(1,128)S(1)}, f32[1,576]{1,0:T(1,128)S(1)}, u32[]{:S(2)}, u32[]{:S(2)}) collective-permute-start(f32[1,576]{1,0:T(1,128)S(1)} %slice.637), channel_id=1, source_target_pairs={{1,0},{2,1},{3,2},{5,4},{6,5},{7,6},{9,8},{10,9},{11,10},{13,12},{... | collective-permute-start | bytes 6920 | tf_op jit(solution)/shard_map/ppermute | solution.py:23
  407.7 8.8 %collective-permute-start.12 = (f32[1,9216]{1,0:T(1,128)}, f32[1,9216]{1,0:T(1,128)}, u32[]{:S(2)}, u32[]{:S(2)}) collective-permute-start(f32[1,9216]{1,0:T(1,128)} %slice_bitcast_fusion.50), channel_id=1, source_target_pairs={{0,4},{4,8},{8,12},{12,0},{1,5},{5,9},{9,13},{13,1},{2,6},{6,10},{... | collective-permute-start | bytes 110600 | tf_op jit(solution)/shard_map/ppermute | solution.py:20
  408.3 8.1 %collective-permute-start.13 = (f32[1,9216]{1,0:T(1,128)}, f32[1,9216]{1,0:T(1,128)}, u32[]{:S(2)}, u32[]{:S(2)}) collective-permute-start(f32[1,9216]{1,0:T(1,128)} %slice_bitcast_fusion.49), channel_id=1, source_target_pairs={{4,0},{8,4},{12,8},{0,12},{5,1},{9,5},{13,9},{1,13},{6,2},{10,6},{... | collective-permute-start | bytes 110600 | tf_op jit(solution)/shard_map/ppermute | solution.py:23
  414.4 2.1 copy-start.8
  419.2 16.2 %collective-permute-start.18 = (f32[1,576]{1,0:T(1,128)S(1)}, f32[1,576]{1,0:T(1,128)S(1)}, u32[]{:S(2)}, u32[]{:S(2)}) collective-permute-start(f32[1,576]{1,0:T(1,128)S(1)} %slice.651), channel_id=1, source_target_pairs={{0,1},{1,2},{2,3},{4,5},{5,6},{6,7},{8,9},{9,10},{10,11},{12,13},{... | collective-permute-start | bytes 6920 | tf_op jit(solution)/shard_map/ppermute | solution.py:20
  423.8 11.9 %collective-permute-start.19 = (f32[1,576]{1,0:T(1,128)S(1)}, f32[1,576]{1,0:T(1,128)S(1)}, u32[]{:S(2)}, u32[]{:S(2)}) collective-permute-start(f32[1,576]{1,0:T(1,128)S(1)} %slice.656), channel_id=1, source_target_pairs={{1,0},{2,1},{3,2},{5,4},{6,5},{7,6},{9,8},{10,9},{11,10},{13,12},{... | collective-permute-start | bytes 6920 | tf_op jit(solution)/shard_map/ppermute | solution.py:23
  425.7 10.9 %collective-permute-start.16 = (f32[1,9216]{1,0:T(1,128)}, f32[1,9216]{1,0:T(1,128)}, u32[]{:S(2)}, u32[]{:S(2)}) collective-permute-start(f32[1,9216]{1,0:T(1,128)} %slice_bitcast_fusion.48), channel_id=1, source_target_pairs={{0,4},{4,8},{8,12},{12,0},{1,5},{5,9},{9,13},{13,1},{2,6},{6,10},{... | collective-permute-start | bytes 110600 | tf_op jit(solution)/shard_map/ppermute | solution.py:20
  426.3 10.3 %copy-start.3 = (f32[72,8,128]{2,0,1:T(8,128)S(1)}, f32[72,8,128]{2,0,1:T(8,128)}, u32[]{:S(2)}) copy-start(f32[72,8,128]{2,0,1:T(8,128)} %fusion.42) | copy-start | bytes 884740
  426.3 10.3 %collective-permute-start.17 = (f32[1,9216]{1,0:T(1,128)}, f32[1,9216]{1,0:T(1,128)}, u32[]{:S(2)}, u32[]{:S(2)}) collective-permute-start(f32[1,9216]{1,0:T(1,128)} %slice_bitcast_fusion.47), channel_id=1, source_target_pairs={{4,0},{8,4},{12,8},{0,12},{5,1},{9,5},{13,9},{1,13},{6,2},{10,6},{... | collective-permute-start | bytes 110600 | tf_op jit(solution)/shard_map/ppermute | solution.py:23
  434.5 2.1 copy-start.9
  439.4 15.4 %collective-permute-start.22 = (f32[1,576]{1,0:T(1,128)S(1)}, f32[1,576]{1,0:T(1,128)S(1)}, u32[]{:S(2)}, u32[]{:S(2)}) collective-permute-start(f32[1,576]{1,0:T(1,128)S(1)} %slice.670), channel_id=1, source_target_pairs={{0,1},{1,2},{2,3},{4,5},{5,6},{6,7},{8,9},{9,10},{10,11},{12,13},{... | collective-permute-start | bytes 6920 | tf_op jit(solution)/shard_map/ppermute | solution.py:20
  443.7 12.4 %copy-start.5 = (f32[72,8,128]{2,0,1:T(8,128)S(1)}, f32[72,8,128]{2,0,1:T(8,128)}, u32[]{:S(2)}) copy-start(f32[72,8,128]{2,0,1:T(8,128)} %fusion.40) | copy-start | bytes 884740
  445.3 9.8 %collective-permute-start.23 = (f32[1,576]{1,0:T(1,128)S(1)}, f32[1,576]{1,0:T(1,128)S(1)}, u32[]{:S(2)}, u32[]{:S(2)}) collective-permute-start(f32[1,576]{1,0:T(1,128)S(1)} %slice.675), channel_id=1, source_target_pairs={{1,0},{2,1},{3,2},{5,4},{6,5},{7,6},{9,8},{10,9},{11,10},{13,12},{... | collective-permute-start | bytes 6920 | tf_op jit(solution)/shard_map/ppermute | solution.py:23
  447.2 8.8 %collective-permute-start.20 = (f32[1,9216]{1,0:T(1,128)}, f32[1,9216]{1,0:T(1,128)}, u32[]{:S(2)}, u32[]{:S(2)}) collective-permute-start(f32[1,9216]{1,0:T(1,128)} %slice_bitcast_fusion.46), channel_id=1, source_target_pairs={{0,4},{4,8},{8,12},{12,0},{1,5},{5,9},{9,13},{13,1},{2,6},{6,10},{... | collective-permute-start | bytes 110600 | tf_op jit(solution)/shard_map/ppermute | solution.py:20
  447.9 8.2 %collective-permute-start.21 = (f32[1,9216]{1,0:T(1,128)}, f32[1,9216]{1,0:T(1,128)}, u32[]{:S(2)}, u32[]{:S(2)}) collective-permute-start(f32[1,9216]{1,0:T(1,128)} %slice_bitcast_fusion.45), channel_id=1, source_target_pairs={{4,0},{8,4},{12,8},{0,12},{5,1},{9,5},{13,9},{1,13},{6,2},{10,6},{... | collective-permute-start | bytes 110600 | tf_op jit(solution)/shard_map/ppermute | solution.py:23
  453.9 2.1 copy-start.10
  458.8 13.9 %collective-permute-start.26 = (f32[1,576]{1,0:T(1,128)S(1)}, f32[1,576]{1,0:T(1,128)S(1)}, u32[]{:S(2)}, u32[]{:S(2)}) collective-permute-start(f32[1,576]{1,0:T(1,128)S(1)} %slice.689), channel_id=1, source_target_pairs={{0,1},{1,2},{2,3},{4,5},{5,6},{6,7},{8,9},{9,10},{10,11},{12,13},{... | collective-permute-start | bytes 6920 | tf_op jit(solution)/shard_map/ppermute | solution.py:20
  463.4 9.6 %collective-permute-start.27 = (f32[1,576]{1,0:T(1,128)S(1)}, f32[1,576]{1,0:T(1,128)S(1)}, u32[]{:S(2)}, u32[]{:S(2)}) collective-permute-start(f32[1,576]{1,0:T(1,128)S(1)} %slice.694), channel_id=1, source_target_pairs={{1,0},{2,1},{3,2},{5,4},{6,5},{7,6},{9,8},{10,9},{11,10},{13,12},{... | collective-permute-start | bytes 6920 | tf_op jit(solution)/shard_map/ppermute | solution.py:23
  465.3 8.6 %collective-permute-start.24 = (f32[1,9216]{1,0:T(1,128)}, f32[1,9216]{1,0:T(1,128)}, u32[]{:S(2)}, u32[]{:S(2)}) collective-permute-start(f32[1,9216]{1,0:T(1,128)} %slice_bitcast_fusion.44), channel_id=1, source_target_pairs={{0,4},{4,8},{8,12},{12,0},{1,5},{5,9},{9,13},{13,1},{2,6},{6,10},{... | collective-permute-start | bytes 110600 | tf_op jit(solution)/shard_map/ppermute | solution.py:20
  465.9 8.0 %collective-permute-start.25 = (f32[1,9216]{1,0:T(1,128)}, f32[1,9216]{1,0:T(1,128)}, u32[]{:S(2)}, u32[]{:S(2)}) collective-permute-start(f32[1,9216]{1,0:T(1,128)} %slice_bitcast_fusion.43), channel_id=1, source_target_pairs={{4,0},{8,4},{12,8},{0,12},{5,1},{9,5},{13,9},{1,13},{6,2},{10,6},{... | collective-permute-start | bytes 110600 | tf_op jit(solution)/shard_map/ppermute | solution.py:23
  471.8 2.1 copy-start.11
  476.7 10.0 %collective-permute-start.30 = (f32[1,576]{1,0:T(1,128)S(1)}, f32[1,576]{1,0:T(1,128)S(1)}, u32[]{:S(2)}, u32[]{:S(2)}) collective-permute-start(f32[1,576]{1,0:T(1,128)S(1)} %slice.708), channel_id=1, source_target_pairs={{0,1},{1,2},{2,3},{4,5},{5,6},{6,7},{8,9},{9,10},{10,11},{12,13},{... | collective-permute-start | bytes 6920 | tf_op jit(solution)/shard_map/ppermute | solution.py:20
  481.0 8.7 %collective-permute-start.28 = (f32[1,9216]{1,0:T(1,128)S(1)}, f32[1,9216]{1,0:T(1,128)S(1)}, u32[]{:S(2)}, u32[]{:S(2)}) collective-permute-start(f32[1,9216]{1,0:T(1,128)S(1)} %slice_bitcast_fusion.42), channel_id=1, source_target_pairs={{0,4},{4,8},{8,12},{12,0},{1,5},{5,9},{9,13},{13,1},{2,6},{6,10},{... | collective-permute-start | bytes 110600 | tf_op jit(solution)/shard_map/ppermute | solution.py:20
  481.1 8.7 %collective-permute-start.29 = (f32[1,9216]{1,0:T(1,128)S(1)}, f32[1,9216]{1,0:T(1,128)S(1)}, u32[]{:S(2)}, u32[]{:S(2)}) collective-permute-start(f32[1,9216]{1,0:T(1,128)S(1)} %slice_bitcast_fusion.41), channel_id=1, source_target_pairs={{4,0},{8,4},{12,8},{0,12},{5,1},{9,5},{13,9},{1,13},{6,2},{10,6},{... | collective-permute-start | bytes 110600 | tf_op jit(solution)/shard_map/ppermute | solution.py:23
  485.2 4.3 collective-permute-start.31
  (2 other events, 2.7 us)
Sparse Core Ops, SparseCore 0:
  290.8 40.3 all-reduce.17
where the time goes:
time: 502 us; the launch traced here: 498 us
  local copies, waits for them, and re-layouts  174 us (35%)
  other arithmetic  139 us (28%)
  starting transfers between devices  85.7 us (17%)
  waiting for transfers between devices  74.8 us (15%)
  between operations  15 us (3%)
  matrix products  10 us (2%)
    scatter-add x1, other arithmetic, per_device(): jnp.zeros((KLEV, STEPS * cells), jnp.float32).at[:, got_segment]  112 us
    psum x1, waiting for transfers between devices, per_device(): binned = lax.psum(local_bins, 'orbit')  40.5 us
    ppermute x16, starting transfers between devices, padded(): lax.ppermute(lax.slice_in_dim(block, 0, width, axis=dim), axis, backward)  39.5 us
    scatter x1, local copies, waits for them, and re-layouts, build_slots(): slot_values = jnp.zeros((kernel.shape[0], owners * capacity), jnp.float32...  37.3 us
    ppermute x16, starting transfers between devices, padded(): lax.ppermute(lax.slice_in_dim(block, block.shape[dim] - width, None, axis...  32.6 us
    all_to_all x1, waiting for transfers between devices, per_device(): lax.all_to_all(send_values, ('lon', 'lat'), split_axis=1, concat_axis=1,...  31.7 us
    gather x1, local copies, waits for them, and re-layouts, build_slots(): sorted_owner = owner_ids[ordering]  23 us
    gather x1, local copies, waits for them, and re-layouts, build_slots(): segment[ordering]  23 us
  transfers between devices with their start and end apart: 35, of which 3 were waited for; matrix products, arithmetic and copies ran while one was open for 20% of the time, Pallas kernels for 0%

commit v1 on v0

v1 whole, which is shorter than its diff:
```python
import functools

import jax
import jax.numpy as jnp
import numpy as np
from jax import lax
from jax.experimental import pallas as pl
from jax.experimental.pallas import tpu as pltpu
from jax.sharding import PartitionSpec as P

STEPS = 8
CLON = 8
CLAT = 128
CELLS = CLON * CLAT
ROWS = 24
CHUNK = 256
F32 = jnp.float32
BF16 = jnp.bfloat16
VMEM_LIMIT = 48 * 1024 * 1024
NT = (((1,), (1,)), ((), ()))


def level_weights(levels, kernel_levels):
    one = np.float32
    heights = np.arange(levels, dtype=np.float32)
    centre = np.clip((heights + one(0.5)) * one(kernel_levels) / one(levels) - one(0.5),
                     one(0), one(kernel_levels - 1))
    knots = np.arange(kernel_levels, dtype=np.float32)
    return np.maximum(one(0), one(1) - np.abs(centre[:, None] - knots[None, :]))


def split(values):
    high = values.astype(BF16)
    return high, (values - high.astype(F32)).astype(BF16)


def pack_kernel(owners, capacity, starts_ref, kernel_ref, residual_ref, owner_ref, segment_ref,
                out_ref, data_ref, place_ref, sorted_ref):
    levels, count = kernel_ref.shape
    chunks = count // CHUNK
    half = data_ref.shape[0] // 2
    high, low = split(kernel_ref[...] * residual_ref[...])
    segment = segment_ref[...]
    spare = jnp.zeros((half - levels - 1, count), F32)
    seg_high = (segment // CLAT * CLAT).astype(F32)
    seg_low = (segment % CLAT).astype(F32)
    data_ref[0:half] = jnp.concatenate(
        [high.astype(F32), seg_high, spare], axis=0).astype(BF16)
    data_ref[half:] = jnp.concatenate(
        [low.astype(F32), seg_low, spare], axis=0).astype(BF16)

    names = lax.broadcasted_iota(jnp.int32, (owners, CHUNK), 0)
    earlier = (lax.broadcasted_iota(jnp.int32, (CHUNK, CHUNK), 0)
               < lax.broadcasted_iota(jnp.int32, (CHUNK, CHUNK), 1)).astype(F32).astype(BF16)
    totals = jnp.zeros((owners, 1), F32)
    for c in range(chunks):
        own = (owner_ref[:, c * CHUNK:(c + 1) * CHUNK] == names).astype(F32)
        totals = totals + jnp.sum(own, axis=1, keepdims=True)
    before = (lax.broadcasted_iota(jnp.int32, (owners, owners), 1)
              < lax.broadcasted_iota(jnp.int32, (owners, owners), 0)).astype(F32)
    carry = jnp.dot(before, jnp.broadcast_to(totals, (owners, CHUNK)),
                    precision=lax.Precision.HIGHEST, preferred_element_type=F32)[:, 0:1]
    for c in range(chunks):
        own = (owner_ref[:, c * CHUNK:(c + 1) * CHUNK] == names).astype(F32)
        inside = jnp.dot(own.astype(BF16), earlier, preferred_element_type=F32)
        place_ref[:, c * CHUNK:(c + 1) * CHUNK] = jnp.sum(
            own * (inside + carry), axis=0, keepdims=True).astype(jnp.int32)
        carry = carry + jnp.sum(own, axis=1, keepdims=True)

    def arrange(block, _):
        base = block * CHUNK
        target = lax.broadcasted_iota(jnp.int32, (CHUNK, count), 0) + base
        chosen = (target == place_ref[...]).astype(F32).astype(BF16)
        got = lax.dot_general(data_ref[...], chosen, NT, preferred_element_type=F32)
        sorted_ref[:, pl.ds(pl.multiple_of(base, CHUNK), CHUNK)] = got[0:ROWS] + got[half:half + ROWS]
        return 0

    lax.fori_loop(0, chunks, arrange, 0)
    sorted_ref[:, count:] = jnp.zeros((ROWS, sorted_ref.shape[1] - count), F32)
    window = capacity + CLAT
    slot = lax.broadcasted_iota(jnp.int32, (ROWS, capacity), 1)
    row = lax.broadcasted_iota(jnp.int32, (ROWS, capacity), 0)

    def hand_out(name, _):
        start = starts_ref[name]
        length = starts_ref[name + 1] - start
        aligned = start // CLAT * CLAT
        run = sorted_ref[:, pl.ds(pl.multiple_of(aligned, CLAT), window)]
        run = pltpu.roll(run, lax.rem(window - (start - aligned), window), 1)[:, 0:capacity]
        out_ref[name] = jnp.where((row == levels) & (slot >= length), -1.0, run)
        return 0

    lax.fori_loop(0, owners, hand_out, 0)


def pack(kernel, residual, owner_block, column, time_step, owners, capacity):
    levels, count = kernel.shape
    owner = owner_block.reshape(1, count)
    segment = (time_step * CELLS + column).reshape(1, count)
    labels = jnp.arange(owners + 1, dtype=jnp.int32)
    starts = jnp.sum((owner < labels[:, None]).astype(jnp.int32), axis=1)
    vmem = pl.BlockSpec(memory_space=pltpu.VMEM)
    return pl.pallas_call(
        functools.partial(pack_kernel, owners, capacity),
        out_shape=jax.ShapeDtypeStruct((owners, ROWS, capacity), F32),
        in_specs=[pl.BlockSpec(memory_space=pltpu.SMEM)] + [vmem] * 4,
        out_specs=vmem,
        scratch_shapes=[
            pltpu.VMEM((64, count), BF16),
            pltpu.VMEM((1, count), jnp.int32),
            pltpu.VMEM((ROWS, count + capacity + CLAT), F32),
        ],
        compiler_params=pltpu.CompilerParams(vmem_limit_bytes=VMEM_LIMIT),
    )(starts, kernel, residual.reshape(1, count), owner, segment)


def bin_kernel(levels, got_ref, out_ref, total_ref):
    source = pl.program_id(0)
    capacity = got_ref.shape[2]
    width = min(capacity, CHUNK)
    half = STEPS * ROWS

    @pl.when(source == 0)
    def _():
        total_ref[...] = jnp.zeros_like(total_ref)

    for piece in range(capacity // width):
        rows = got_ref[0, :, piece * width:(piece + 1) * width]
        segment = rows[levels:levels + 1].astype(jnp.int32)

        @pl.when(jnp.max(rows[levels:levels + 1]) >= 0.0)
        def _():
            step = jnp.broadcast_to(segment >> 10, (ROWS, width))
            cell = segment & (CELLS - 1)
            place = lax.broadcasted_iota(jnp.int32, (CELLS, width), 0)
            chosen = (place == cell).astype(F32).astype(BF16)
            taken = jnp.concatenate(
                [jnp.where(step == j, rows, 0.0) for j in range(STEPS)], axis=0)
            high = taken.astype(BF16)
            low = (taken - high.astype(F32)).astype(BF16)
            total_ref[...] += lax.dot_general(
                jnp.concatenate([high, low], axis=0), chosen, NT, preferred_element_type=F32)

    @pl.when(source == pl.num_programs(0) - 1)
    def _():
        for i in range(CLON):
            part = (total_ref[0:half, i * CLAT:(i + 1) * CLAT]
                    + total_ref[half:, i * CLAT:(i + 1) * CLAT])
            for j in range(STEPS):
                out_ref[j, :, i, :] = part[j * ROWS:j * ROWS + levels]


def bin_soundings(got, levels):
    owners, rows, capacity = got.shape
    return pl.pallas_call(
        functools.partial(bin_kernel, levels),
        out_shape=jax.ShapeDtypeStruct((STEPS, levels, CLON, CLAT), F32),
        grid=(owners,),
        in_specs=[pl.BlockSpec((1, rows, capacity), lambda i: (i, 0, 0))],
        out_specs=pl.BlockSpec((STEPS, levels, CLON, CLAT), lambda i: (0, 0, 0, 0)),
        scratch_shapes=[pltpu.VMEM((2 * STEPS * ROWS, CELLS), F32)],
        compiler_params=pltpu.CompilerParams(vmem_limit_bytes=VMEM_LIMIT),
    )(got)


def steps_kernel(orbits, lons, lats, weights, bins_ref, horizontal_ref, vertical_ref,
                 adjoint_ref, flux_ref, other_ref, term_ref, diagonal_ref,
                 lon_out, lon_in, lat_out, lat_in,
                 orbit_send, orbit_recv, edge_send, edge_recv):
    levels = adjoint_ref.shape[0]
    lon, lat, orbit = lax.axis_index("lon"), lax.axis_index("lat"), lax.axis_index("orbit")
    east, west = lax.rem(lon + 1, lons), lax.rem(lon + lons - 1, lons)
    partner = 1 - orbit
    mesh_id = pl.DeviceIdType.MESH
    barrier = pltpu.get_barrier_semaphore()
    pl.semaphore_signal(barrier, inc=1, device_id={"lon": east}, device_id_type=mesh_id)
    pl.semaphore_signal(barrier, inc=1, device_id={"lon": west}, device_id_type=mesh_id)
    pl.semaphore_signal(barrier, inc=1, device_id={"orbit": partner}, device_id_type=mesh_id)

    @pl.when(lat < lats - 1)
    def _():
        pl.semaphore_signal(barrier, inc=1, device_id={"lat": lat + 1}, device_id_type=mesh_id)

    @pl.when(lat > 0)
    def _():
        pl.semaphore_signal(barrier, inc=1, device_id={"lat": lat - 1}, device_id_type=mesh_id)

    peers = 3 + jnp.where(lat > 0, 1, 0) + jnp.where(lat < lats - 1, 1, 0)
    pl.semaphore_wait(barrier, peers)

    def orbit_copy(j):
        return pltpu.make_async_remote_copy(
            src_ref=bins_ref.at[j], dst_ref=other_ref.at[j],
            send_sem=orbit_send.at[j], recv_sem=orbit_recv.at[j],
            device_id={"orbit": partner}, device_id_type=mesh_id)

    def edge_copy(t, side):
        out, into = (lon_out, lon_in) if side < 2 else (lat_out, lat_in)
        device = ({"lon": east}, {"lon": west}, {"lat": lat + 1}, {"lat": lat - 1})[side]
        return pltpu.make_async_remote_copy(
            src_ref=out.at[side % 2, t], dst_ref=into.at[side % 2, t],
            send_sem=edge_send.at[side, t], recv_sem=edge_recv.at[side, t],
            device_id=device, device_id_type=mesh_id)

    def begin(t, _):
        orbit_copy(STEPS - 1 - t).start()
        return 0

    lax.fori_loop(0, STEPS, begin, 0)

    @pl.when(lat == 0)
    def _():
        lat_in[0] = jnp.zeros(lat_in.shape[1:], F32)

    @pl.when(lat == lats - 1)
    def _():
        lat_in[1] = jnp.zeros(lat_in.shape[1:], F32)

    diagonal_ref[...] = (1.0 - horizontal_ref[0] - horizontal_ref[1]
                         - horizontal_ref[2] - horizontal_ref[3])
    adjoint_ref[...] = jnp.zeros_like(adjoint_ref)
    flux_ref[...] = jnp.zeros_like(flux_ref)
    shape = adjoint_ref.shape
    lane = lax.broadcasted_iota(jnp.int32, shape, 2)
    sub = lax.broadcasted_iota(jnp.int32, shape, 1)
    level = lax.broadcasted_iota(jnp.int32, shape, 0)

    def advance(t, _):
        j = STEPS - 1 - t
        orbit_copy(j).wait_recv()
        bins = bins_ref[j] + other_ref[j]
        forcing = []
        for l in range(levels):
            parts = [bins[k:k + 1] * float(weights[l, k]) for k in np.nonzero(weights[l])[0]]
            forcing.append(functools.reduce(lambda a, b: a + b, parts))
        forced = adjoint_ref[...] + jnp.concatenate(forcing, axis=0)
        up = vertical_ref[...] * (forced[1:] - forced[:-1])
        none = jnp.zeros((1, CLON, CLAT), F32)
        mixed = (forced + jnp.concatenate([up, none], axis=0)
                 - jnp.concatenate([none, up], axis=0))
        term_ref[0] = horizontal_ref[0] * mixed
        term_ref[1] = horizontal_ref[1] * mixed
        north = horizontal_ref[2] * mixed
        south = horizontal_ref[3] * mixed
        lon_out[0, t] = term_ref[0, :, CLON - 1, :]
        lon_out[1, t] = term_ref[1, :, 0, :]
        edge_copy(t, 0).start()
        edge_copy(t, 1).start()
        lat_out[0, t] = jnp.sum(jnp.where(
            lane == level, jnp.broadcast_to(north[:, :, CLAT - 1:CLAT], shape), 0.0), axis=0)
        lat_out[1, t] = jnp.sum(jnp.where(
            lane == level, jnp.broadcast_to(south[:, :, 0:1], shape), 0.0), axis=0)

        @pl.when(lat < lats - 1)
        def _():
            edge_copy(t, 2).start()

        @pl.when(lat > 0)
        def _():
            edge_copy(t, 3).start()

        inside = (diagonal_ref[...] * mixed
                  + jnp.where(sub == 0, 0.0, pltpu.roll(term_ref[0], 1, 1))
                  + jnp.where(sub == CLON - 1, 0.0, pltpu.roll(term_ref[1], CLON - 1, 1))
                  + jnp.where(lane == 0, 0.0, pltpu.roll(north, 1, 2))
                  + jnp.where(lane == CLAT - 1, 0.0, pltpu.roll(south, CLAT - 1, 2)))
        adjoint_ref[...] = inside

        @pl.when(lat > 0)
        def _():
            edge_copy(t, 2).wait_recv()

        @pl.when(lat < lats - 1)
        def _():
            edge_copy(t, 3).wait_recv()

        edge_copy(t, 0).wait_recv()
        edge_copy(t, 1).wait_recv()
        low = jnp.sum(jnp.where(lane == level, lat_in[0, t][None], 0.0), axis=2, keepdims=True)
        high = jnp.sum(jnp.where(lane == level, lat_in[1, t][None], 0.0), axis=2, keepdims=True)
        first = lon_in[0, t].reshape(levels, 1, CLAT)
        last = lon_in[1, t].reshape(levels, 1, CLAT)
        result = (adjoint_ref[...]
                  + jnp.where(sub == 0, first, 0.0) + jnp.where(sub == CLON - 1, last, 0.0)
                  + jnp.where(lane == 0, low, 0.0) + jnp.where(lane == CLAT - 1, high, 0.0))
        adjoint_ref[...] = result
        flux_ref[...] += result[0]
        return 0

    lax.fori_loop(0, STEPS, advance, 0)

    def finish(t, _):
        orbit_copy(t).wait_send()
        edge_copy(t, 0).wait_send()
        edge_copy(t, 1).wait_send()

        @pl.when(lat < lats - 1)
        def _():
            edge_copy(t, 2).wait_send()

        @pl.when(lat > 0)
        def _():
            edge_copy(t, 3).wait_send()

        return 0

    lax.fori_loop(0, STEPS, finish, 0)


def transport(bins, horizontal, vertical):
    levels = horizontal.shape[1]
    kernel_levels = bins.shape[1]
    orbits, lons, lats = (lax.axis_size(name) for name in ("orbit", "lon", "lat"))
    vmem = pl.BlockSpec(memory_space=pltpu.VMEM)
    block = (levels, CLON, CLAT)
    return pl.pallas_call(
        functools.partial(steps_kernel, orbits, lons, lats, level_weights(levels, kernel_levels)),
        out_shape=(jax.ShapeDtypeStruct(block, F32), jax.ShapeDtypeStruct((CLON, CLAT), F32)),
        in_specs=[vmem] * 3,
        out_specs=(vmem, vmem),
        scratch_shapes=[
            pltpu.VMEM(bins.shape, F32),
            pltpu.VMEM((2,) + block, F32),
            pltpu.VMEM(block, F32),
            pltpu.VMEM((2, STEPS, levels, CLAT), F32),
            pltpu.VMEM((2, STEPS, levels, CLAT), F32),
            pltpu.VMEM((2, STEPS, CLON, CLAT), F32),
            pltpu.VMEM((2, STEPS, CLON, CLAT), F32),
            pltpu.SemaphoreType.DMA((STEPS,)),
            pltpu.SemaphoreType.DMA((STEPS,)),
            pltpu.SemaphoreType.DMA((4, STEPS)),
            pltpu.SemaphoreType.DMA((4, STEPS)),
        ],
        compiler_params=pltpu.CompilerParams(
            collective_id=0, has_side_effects=True, vmem_limit_bytes=VMEM_LIMIT),
    )(bins, horizontal, vertical)


def per_device(kernel, residual, owner_block, column, time_step, horizontal, vertical):
    owners = lax.axis_size("lon") * lax.axis_size("lat")
    capacity = 4 * kernel.shape[1] // owners
    slots = pack(kernel, residual, owner_block, column, time_step, owners, capacity)
    got = lax.all_to_all(slots, ("lon", "lat"), split_axis=0, concat_axis=0, tiled=True)
    return transport(bin_soundings(got, kernel.shape[0]), horizontal, vertical)


def solution(mesh):
    placed = (
        P(None, ("orbit", "lon", "lat")),
        P(("orbit", "lon", "lat")),
        P(("orbit", "lon", "lat"), None),
        P(("orbit", "lon", "lat")),
        P(("orbit", "lon", "lat")),
        P(None, None, "lon", "lat"),
        P(None, "lon", "lat"),
    )
    return jax.shard_map(
        per_device,
        mesh=mesh,
        in_specs=placed,
        out_specs=(P(None, "lon", "lat"), P("lon", "lat")),
        check_vma=False,
    )
```

time: 502 us -> 143 us (0.28)
  local copies, waits for them, and re-layouts: 174 us -> 3.74 us
  other arithmetic: 139 us -> 1.62 us
  Pallas kernels: 0 us -> 93.1 us
  starting transfers between devices: 85.7 us -> 0 us
  waiting for transfers between devices: 74.8 us -> 0 us
  blocking collectives: 0 us -> 43.2 us
  between operations: 15 us -> 0.67 us
  matrix products: 10 us -> 0 us
    scatter-add x1 -> x0, other arithmetic: 112 us -> none  [per_device(): jnp.zeros((KLEV, STEPS * cells), jnp.float32).at[:, got_segment]]
    pallas_call x0 -> x3, Pallas kernels: none -> 93.1 us  [the longest x1 62.3 us: transport(): pl.pallas_call(functools.partial(steps_kernel, orbits, lons, lats, level_...]
    ppermute x32 -> x0, starting transfers between devices: 72.1 us -> none  [the longest x16 39.5 us: padded(): lax.ppermute(lax.slice_in_dim(block, 0, width, axis=dim), axis, backward)]
    scatter x2 -> x0, local copies, waits for them, and re-layouts: 53.4 us -> none  [the longest x1 37.3 us: build_slots(): slot_values = jnp.zeros((kernel.shape[0], owners * capacity), jnp.float32...]
    gather x2 -> x0, local copies, waits for them, and re-layouts: 46.1 us -> none  [the longest x1 23 us: build_slots(): sorted_owner = owner_ids[ordering]]
    all_to_all x0 -> x1, blocking collectives: none -> 43.2 us  [per_device(): lax.all_to_all(slots, ('lon', 'lat'), split_axis=0, concat_axis=0, tiled=...]
    psum x1 -> x0, waiting for transfers between devices: 40.5 us -> none  [per_device(): binned = lax.psum(local_bins, 'orbit')]
    slice x65 -> x0, local copies, waits for them, and re-layouts: 36.5 us -> none  [the longest x16 8.24 us: padded(): lax.slice_in_dim(block, 0, width, axis=dim)]
  transfers between devices with their start and end apart: 35 -> 0, of which waited for: 3 -> 0; matrix products, arithmetic and copies ran while one was open for 20% -> 0% of each run, Pallas kernels for 0% -> 0%
where the time goes in v1:
time: 143 us; the launch traced here: 142 us
  Pallas kernels  93.1 us (65%)
  blocking collectives  43.2 us (30%)
  local copies, waits for them, and re-layouts  3.74 us (3%)
  other arithmetic  1.62 us (1%)
    pallas_call x1, Pallas kernels, transport(): pl.pallas_call(functools.partial(steps_kernel, orbits, lons, lats, level_...  62.3 us
    all_to_all x1, blocking collectives, per_device(): lax.all_to_all(slots, ('lon', 'lat'), split_axis=0, concat_axis=0, tiled=...  43.2 us
    pallas_call x1, Pallas kernels, bin_soundings(): pl.pallas_call(functools.partial(bin_kernel, levels), out_shape=jax.Shape...  15.6 us
    pallas_call x1, Pallas kernels, pack(): pl.pallas_call(functools.partial(pack_kernel, owners, capacity), out_shap...  15.2 us
    unnamed x12, local copies, waits for them, and re-layouts  3.74 us

profile of v1, /device:TPU:0, one launch (start us, length us, event | category | flops | bytes accessed | tf_op | source)
XLA Modules:
  0.0 142.4 jit_solution(15373756512261708637)
XLA Ops:
  0.6 0.9 convert_reduce_fusion.starts_ref
  1.5 0.7 multiply_add_fusion
  2.2 0.0 copy-start.1
  2.2 1.0 copy-done.1
  3.2 0.0 copy-start.3
  3.2 0.7 copy-done.3
  4.0 0.0 copy-start.4
  4.0 0.7 copy-done.4
  4.7 15.2 %shard_map.86 = f32[16,24,1024]{2,1,0:T(8,128)S(1)} custom-call(s32[17]{0:T(128)S(1)} %convert_reduce_fusion.starts_ref, f32[20,4096]{1,0:T(8,128)S(1)} %copy-done.1, f32[1,4096]{1,0:T(1,128)S(1)} %bitcast.7, s32[1,4096]{1,0:T(1,128)S(1)} %bitcast.6, s32[1,4096]{1,0:T(1,128)S(1)} %bitcast.4), custom_call_target="tpu_custom_call" | custom-call | tf_op jit(solution)/shard_map/pallas_call | solution.py:103
  19.9 43.2 %all_to_all.5.got_ref = f32[16,24,1024]{2,1,0:T(8,128)S(1)} all-to-all(f32[16,24,1024]{2,1,0:T(8,128)S(1)} %shard_map.86), channel_id=1, replica_groups=mesh['orbit'=2,'lon'=4,'lat'=4] {'lon','lat'}, dimensions={0} | all-to-all | bytes 3145728 | tf_op jit(solution)/shard_map/all_to_all | solution.py:343
  63.2 0.0 copy-start
  63.2 0.0 copy-start.2
  63.2 15.6 %shard_map.87.bins_ref = f32[8,20,8,128]{3,2,1,0:T(8,128)S(1)} custom-call(f32[16,24,1024]{2,1,0:T(8,128)S(1)} %all_to_all.5.got_ref), custom_call_target="tpu_custom_call" | custom-call | tf_op jit(solution)/shard_map/pallas_call | solution.py:155
  78.8 0.0 copy-done
  78.8 0.0 copy-done.2
  78.8 62.3 %shard_map.88 = (f32[72,8,128]{2,1,0:T(8,128)S(1)}, f32[8,128]{1,0:T(8,128)S(1)}) custom-call(f32[8,20,8,128]{3,2,1,0:T(8,128)S(1)} %shard_map.87.bins_ref, f32[4,72,8,128]{3,2,1,0:T(8,128)S(1)} %copy-done, f32[71,8,128]{2,1,0:T(8,128)S(1)} %copy-done.2), custom_call_target="tpu_custom_call" | custom-call | tf_op jit(solution)/shard_map/pallas_call | solution.py:316
  141.0 0.7 copy.11
  141.8 0.6 copy.12
Async XLA Ops:
  2.2 1.0 copy-start.1
  3.2 0.7 copy-start.3
  4.0 0.7 copy-start.4
  63.2 15.6 %copy-start = (f32[4,72,8,128]{3,2,1,0:T(8,128)S(1)}, f32[4,72,8,128]{3,2,1,0:T(8,128)}, u32[]{:S(2)}) copy-start(f32[4,72,8,128]{3,2,1,0:T(8,128)} %horizontal_ref.1) | copy-start | bytes 3538948
  63.2 15.6 %copy-start.2 = (f32[71,8,128]{2,1,0:T(8,128)S(1)}, f32[71,8,128]{2,1,0:T(8,128)}, u32[]{:S(2)}) copy-start(f32[71,8,128]{2,1,0:T(8,128)} %vertical_ref.1) | copy-start | bytes 872452

commit v2 on v1

--- a/solution.py
+++ b/solution.py
@@ -87,7 +87,7 @@
         aligned = start // CLAT * CLAT
         run = sorted_ref[:, pl.ds(pl.multiple_of(aligned, CLAT), window)]
         run = pltpu.roll(run, lax.rem(window - (start - aligned), window), 1)[:, 0:capacity]
-        out_ref[name] = jnp.where((row == levels) & (slot >= length), -1.0, run)
+        out_ref[name] = jnp.where((row == levels) & (slot >= length), -1.0, run)[0:levels + 1]
         return 0
 
     lax.fori_loop(0, owners, hand_out, 0)
@@ -102,7 +102,7 @@
     vmem = pl.BlockSpec(memory_space=pltpu.VMEM)
     return pl.pallas_call(
         functools.partial(pack_kernel, owners, capacity),
-        out_shape=jax.ShapeDtypeStruct((owners, ROWS, capacity), F32),
+        out_shape=jax.ShapeDtypeStruct((owners, levels + 1, capacity), F32),
         in_specs=[pl.BlockSpec(memory_space=pltpu.SMEM)] + [vmem] * 4,
         out_specs=vmem,
         scratch_shapes=[
@@ -114,53 +114,95 @@
     )(starts, kernel, residual.reshape(1, count), owner, segment)
 
 
-def bin_kernel(levels, got_ref, out_ref, total_ref):
-    source = pl.program_id(0)
-    capacity = got_ref.shape[2]
-    width = min(capacity, CHUNK)
+def bin_kernel(levels, lons, lats, slots_ref, out_ref, got_ref, total_ref, send_sem, recv_sem):
+    owners, _, capacity = slots_ref.shape
+    lon, lat = lax.axis_index("lon"), lax.axis_index("lat")
+    mesh_id = pl.DeviceIdType.MESH
     half = STEPS * ROWS
-
-    @pl.when(source == 0)
-    def _():
-        total_ref[...] = jnp.zeros_like(total_ref)
-
-    for piece in range(capacity // width):
-        rows = got_ref[0, :, piece * width:(piece + 1) * width]
-        segment = rows[levels:levels + 1].astype(jnp.int32)
-
-        @pl.when(jnp.max(rows[levels:levels + 1]) >= 0.0)
-        def _():
+    width = min(capacity, 2 * CHUNK)
+
+    def peer(d):
+        return lax.rem(lon + d // lats, lons), lax.rem(lat + lax.rem(d, lats), lats)
+
+    def slot_copy(d):
+        to_lon, to_lat = peer(d)
+        return pltpu.make_async_remote_copy(
+            src_ref=slots_ref.at[to_lon * lats + to_lat], dst_ref=got_ref.at[d],
+            send_sem=send_sem.at[d], recv_sem=recv_sem.at[d],
+            device_id={"lon": to_lon, "lat": to_lat}, device_id_type=mesh_id)
+
+    barrier = pltpu.get_barrier_semaphore()
+
+    def greet(d, _):
+        to_lon, to_lat = peer(d)
+        pl.semaphore_signal(barrier, inc=1, device_id={"lon": to_lon, "lat": to_lat},
+                            device_id_type=mesh_id)
+        return 0
+
+    lax.fori_loop(1, owners, greet, 0)
+    pl.semaphore_wait(barrier, owners - 1)
+
+    def begin(d, _):
+        slot_copy(d).start()
+        return 0
+
+    lax.fori_loop(1, owners, begin, 0)
+    total_ref[...] = jnp.zeros_like(total_ref)
+    got_ref[0] = slots_ref[lon * lats + lat]
+
+    def collect(d, _):
+        @pl.when(d > 0)
+        def _():
+            slot_copy(d).wait_recv()
+
+        for piece in range(capacity // width):
+            rows = got_ref[d, :, piece * width:(piece + 1) * width]
+            segment = rows[levels:levels + 1].astype(jnp.int32)
+            values = jnp.concatenate(
+                [rows[0:levels], jnp.zeros((ROWS - levels, width), F32)], axis=0)
             step = jnp.broadcast_to(segment >> 10, (ROWS, width))
             cell = segment & (CELLS - 1)
             place = lax.broadcasted_iota(jnp.int32, (CELLS, width), 0)
             chosen = (place == cell).astype(F32).astype(BF16)
             taken = jnp.concatenate(
-                [jnp.where(step == j, rows, 0.0) for j in range(STEPS)], axis=0)
+                [jnp.where(step == j, values, 0.0) for j in range(STEPS)], axis=0)
             high = taken.astype(BF16)
             low = (taken - high.astype(F32)).astype(BF16)
             total_ref[...] += lax.dot_general(
                 jnp.concatenate([high, low], axis=0), chosen, NT, preferred_element_type=F32)
-
-    @pl.when(source == pl.num_programs(0) - 1)
-    def _():
-        for i in range(CLON):
-            part = (total_ref[0:half, i * CLAT:(i + 1) * CLAT]
-                    + total_ref[half:, i * CLAT:(i + 1) * CLAT])
-            for j in range(STEPS):
-                out_ref[j, :, i, :] = part[j * ROWS:j * ROWS + levels]
-
-
-def bin_soundings(got, levels):
-    owners, rows, capacity = got.shape
+        return 0
+
+    lax.fori_loop(0, owners, collect, 0)
+    for i in range(CLON):
+        part = (total_ref[0:half, i * CLAT:(i + 1) * CLAT]
+                + total_ref[half:, i * CLAT:(i + 1) * CLAT])
+        for j in range(STEPS):
+            out_ref[j, :, i, :] = part[j * ROWS:j * ROWS + levels]
+
+    def finish(d, _):
+        slot_copy(d).wait_send()
+        return 0
+
+    lax.fori_loop(1, owners, finish, 0)
+
+
+def bin_soundings(slots, levels):
+    lons, lats = lax.axis_size("lon"), lax.axis_size("lat")
+    vmem = pl.BlockSpec(memory_space=pltpu.VMEM)
     return pl.pallas_call(
-        functools.partial(bin_kernel, levels),
+        functools.partial(bin_kernel, levels, lons, lats),
         out_shape=jax.ShapeDtypeStruct((STEPS, levels, CLON, CLAT), F32),
-        grid=(owners,),
-        in_specs=[pl.BlockSpec((1, rows, capacity), lambda i: (i, 0, 0))],
-        out_specs=pl.BlockSpec((STEPS, levels, CLON, CLAT), lambda i: (0, 0, 0, 0)),
-        scratch_shapes=[pltpu.VMEM((2 * STEPS * ROWS, CELLS), F32)],
-        compiler_params=pltpu.CompilerParams(vmem_limit_bytes=VMEM_LIMIT),
-    )(got)
+        in_specs=[vmem],
+        out_specs=vmem,
+        scratch_shapes=[
+            pltpu.VMEM(slots.shape, F32),
+            pltpu.VMEM((2 * STEPS * ROWS, CELLS), F32),
+            pltpu.SemaphoreType.DMA((lons * lats,)),
+            pltpu.SemaphoreType.DMA((lons * lats,)),
+        ],
+        compiler_params=pltpu.CompilerParams(
+            collective_id=1, has_side_effects=True, vmem_limit_bytes=VMEM_LIMIT),
+    )(slots)
 
 
 def steps_kernel(orbits, lons, lats, weights, bins_ref, horizontal_ref, vertical_ref,
@@ -340,8 +382,7 @@
     owners = lax.axis_size("lon") * lax.axis_size("lat")
     capacity = 4 * kernel.shape[1] // owners
     slots = pack(kernel, residual, owner_block, column, time_step, owners, capacity)
-    got = lax.all_to_all(slots, ("lon", "lat"), split_axis=0, concat_axis=0, tiled=True)
-    return transport(bin_soundings(got, kernel.shape[0]), horizontal, vertical)
+    return transport(bin_soundings(slots, kernel.shape[0]), horizontal, vertical)
 
 
 def solution(mesh):

time: 143 us -> 113 us (0.79)
  blocking collectives: 43.2 us -> 0 us
  Pallas kernels: 93.1 us -> 106 us
    all_to_all x1 -> x0, blocking collectives: 43.2 us -> none  [per_device(): lax.all_to_all(slots, ('lon', 'lat'), split_axis=0, concat_axis=0, tiled=...]
    pallas_call x1, Pallas kernels: 15.6 us -> 38.8 us  [bin_soundings(): pl.pallas_call(functools.partial(bin_kernel, levels, lons, lats), out_sha...]
    pallas_call x1, Pallas kernels: 62.3 us -> 52.2 us  [transport(): pl.pallas_call(functools.partial(steps_kernel, orbits, lons, lats, level_...]
where the time goes in v2:
time: 113 us; the launch traced here: 112 us
  Pallas kernels  106 us (94%)
  local copies, waits for them, and re-layouts  3.75 us (3%)
  other arithmetic  1.62 us (1%)
    pallas_call x1, Pallas kernels, transport(): pl.pallas_call(functools.partial(steps_kernel, orbits, lons, lats, level_...  52.2 us
    pallas_call x1, Pallas kernels, bin_soundings(): pl.pallas_call(functools.partial(bin_kernel, levels, lons, lats), out_sha...  38.8 us
    pallas_call x1, Pallas kernels, pack(): pl.pallas_call(functools.partial(pack_kernel, owners, capacity), out_shap...  15.2 us
    unnamed x12, local copies, waits for them, and re-layouts  3.75 us

profile of v2, /device:TPU:0, one launch (start us, length us, event | category | flops | bytes accessed | tf_op | source)
XLA Modules:
  0.0 112.3 jit_solution(988294972774293215)
XLA Ops:
  0.6 0.9 convert_reduce_fusion.starts_ref
  1.5 0.7 multiply_add_fusion
  2.2 0.0 copy-start.1
  2.2 1.0 copy-done.1
  3.2 0.0 copy-start.3
  3.2 0.7 copy-done.3
  4.0 0.0 copy-start.4
  4.0 0.7 copy-done.4
  4.7 15.2 %shard_map.86.slots_ref = f32[16,21,1024]{2,1,0:T(8,128)S(1)} custom-call(s32[17]{0:T(128)S(1)} %convert_reduce_fusion.starts_ref, f32[20,4096]{1,0:T(8,128)S(1)} %copy-done.1, f32[1,4096]{1,0:T(1,128)S(1)} %bitcast.7, s32[1,4096]{1,0:T(1,128)S(1)} %bitcast.6, s32[1,4096]{1,0:T(1,128)S(1)} %bitcast.4), custom_call_target="tpu_custom_call" | custom-call | tf_op jit(solution)/shard_map/pallas_call | solution.py:103
  19.9 0.0 copy-start
  19.9 0.0 copy-start.2
  19.9 38.8 %shard_map.87.bins_ref = f32[8,20,8,128]{3,2,1,0:T(8,128)S(1)} custom-call(f32[16,21,1024]{2,1,0:T(8,128)S(1)} %shard_map.86.slots_ref), custom_call_target="tpu_custom_call" | custom-call | tf_op jit(solution)/shard_map/pallas_call | solution.py:192
  58.8 0.0 copy-done
  58.8 0.0 copy-done.2
  58.8 52.2 %shard_map.88 = (f32[72,8,128]{2,1,0:T(8,128)S(1)}, f32[8,128]{1,0:T(8,128)S(1)}) custom-call(f32[8,20,8,128]{3,2,1,0:T(8,128)S(1)} %shard_map.87.bins_ref, f32[4,72,8,128]{3,2,1,0:T(8,128)S(1)} %copy-done, f32[71,8,128]{2,1,0:T(8,128)S(1)} %copy-done.2), custom_call_target="tpu_custom_call" | custom-call | tf_op jit(solution)/shard_map/pallas_call | solution.py:358
  111.0 0.7 copy.11
  111.7 0.6 copy.12
Async XLA Ops:
  2.2 1.0 copy-start.1
  3.2 0.7 copy-start.3
  4.0 0.7 copy-start.4
  19.9 38.9 %copy-start = (f32[4,72,8,128]{3,2,1,0:T(8,128)S(1)}, f32[4,72,8,128]{3,2,1,0:T(8,128)}, u32[]{:S(2)}) copy-start(f32[4,72,8,128]{3,2,1,0:T(8,128)} %horizontal_ref.1) | copy-start | bytes 3538948
  19.9 38.9 %copy-start.2 = (f32[71,8,128]{2,1,0:T(8,128)S(1)}, f32[71,8,128]{2,1,0:T(8,128)}, u32[]{:S(2)}) copy-start(f32[71,8,128]{2,1,0:T(8,128)} %vertical_ref.1) | copy-start | bytes 872452

commit v3 on v2

--- a/solution.py
+++ b/solution.py
@@ -206,8 +206,8 @@
 
 
 def steps_kernel(orbits, lons, lats, weights, bins_ref, horizontal_ref, vertical_ref,
-                 adjoint_ref, flux_ref, other_ref, term_ref, diagonal_ref,
-                 lon_out, lon_in, lat_out, lat_in,
+                 adjoint_ref, flux_ref, other_ref, forced_ref, mixed_ref, diagonal_ref, weight_ref,
+                 edge_ref, lon_out, lon_in, lat_out, lat_in,
                  orbit_send, orbit_recv, edge_send, edge_recv):
     levels = adjoint_ref.shape[0]
     lon, lat, orbit = lax.axis_index("lon"), lax.axis_index("lat"), lax.axis_index("orbit")
@@ -258,40 +258,72 @@
     def _():
         lat_in[1] = jnp.zeros(lat_in.shape[1:], F32)
 
-    diagonal_ref[...] = (1.0 - horizontal_ref[0] - horizontal_ref[1]
-                         - horizontal_ref[2] - horizontal_ref[3])
-    adjoint_ref[...] = jnp.zeros_like(adjoint_ref)
+    part = (8, CLON, CLAT)
+    lane = lax.broadcasted_iota(jnp.int32, part, 2)
+    sub = lax.broadcasted_iota(jnp.int32, part, 1)
+    level = lax.broadcasted_iota(jnp.int32, part, 0)
+    chunks = range(0, levels, 8)
+    pairs = CLAT // 2
+
+    def gather_edge(total, values, side, first):
+        column = values[:, :, CLAT - 1:CLAT] if side == 0 else values[:, :, 0:1]
+        where = (2 * first - side) % CLAT
+        place = (where + 2 * level) & (CLAT - 1)
+        mine = jnp.sum(jnp.where(lane == place, jnp.broadcast_to(column, part), 0.0), axis=0)
+        group = first // pairs
+        total[group] = mine if total[group] is None else total[group] + mine
+
+    groups = lat_in.shape[2]
+    edge_weight = [[None] * groups, [None] * groups]
+    for a in chunks:
+        here = slice(a, a + 8)
+        h = [horizontal_ref[d, here] for d in range(4)]
+        diagonal_ref[here] = 1.0 - h[0] - h[1] - h[2] - h[3]
+        weight_ref[0, here] = jnp.where(sub == 0, 0.0, pltpu.roll(h[0], 1, 1))
+        weight_ref[1, here] = jnp.where(sub == CLON - 1, 0.0, pltpu.roll(h[1], CLON - 1, 1))
+        weight_ref[2, here] = jnp.where(lane == 0, 0.0, pltpu.roll(h[2], 1, 2))
+        weight_ref[3, here] = jnp.where(lane == CLAT - 1, 0.0, pltpu.roll(h[3], CLAT - 1, 2))
+        gather_edge(edge_weight[0], h[2], 0, a)
+        gather_edge(edge_weight[1], h[3], 1, a)
+    for side in range(2):
+        for g in range(groups):
+            edge_ref[side, g] = edge_weight[side][g]
+
+    def force(bins, a):
+        forcing = []
+        for l in range(a, a + 8):
+            parts = [bins[k:k + 1] * float(weights[l, k]) for k in np.nonzero(weights[l])[0]]
+            forcing.append(functools.reduce(lambda x, y: x + y, parts))
+        return jnp.concatenate(forcing, axis=0)
+
+    orbit_copy(STEPS - 1).wait_recv()
+    bins = bins_ref[STEPS - 1] + other_ref[STEPS - 1]
+    for a in chunks:
+        forced_ref[a:a + 8] = force(bins, a)
     flux_ref[...] = jnp.zeros_like(flux_ref)
-    shape = adjoint_ref.shape
-    lane = lax.broadcasted_iota(jnp.int32, shape, 2)
-    sub = lax.broadcasted_iota(jnp.int32, shape, 1)
-    level = lax.broadcasted_iota(jnp.int32, shape, 0)
+    none = jnp.zeros((1, CLON, CLAT), F32)
 
     def advance(t, _):
-        j = STEPS - 1 - t
-        orbit_copy(j).wait_recv()
-        bins = bins_ref[j] + other_ref[j]
-        forcing = []
-        for l in range(levels):
-            parts = [bins[k:k + 1] * float(weights[l, k]) for k in np.nonzero(weights[l])[0]]
-            forcing.append(functools.reduce(lambda a, b: a + b, parts))
-        forced = adjoint_ref[...] + jnp.concatenate(forcing, axis=0)
-        up = vertical_ref[...] * (forced[1:] - forced[:-1])
-        none = jnp.zeros((1, CLON, CLAT), F32)
-        mixed = (forced + jnp.concatenate([up, none], axis=0)
-                 - jnp.concatenate([none, up], axis=0))
-        term_ref[0] = horizontal_ref[0] * mixed
-        term_ref[1] = horizontal_ref[1] * mixed
-        north = horizontal_ref[2] * mixed
-        south = horizontal_ref[3] * mixed
-        lon_out[0, t] = term_ref[0, :, CLON - 1, :]
-        lon_out[1, t] = term_ref[1, :, 0, :]
+        edges = [[None] * groups, [None] * groups]
+        for a in chunks:
+            low, high = max(a - 1, 0), min(a + 9, levels)
+            forced = forced_ref[low:high]
+            up = vertical_ref[low:high - 1] * (forced[1:] - forced[:-1])
+            if a == 0:
+                up = jnp.concatenate([none, up], axis=0)
+            if a + 8 == levels:
+                up = jnp.concatenate([up, none], axis=0)
+            mixed = forced_ref[a:a + 8] + up[1:] - up[:-1]
+            mixed_ref[a:a + 8] = mixed
+            gather_edge(edges[0], mixed, 0, a)
+            gather_edge(edges[1], mixed, 1, a)
+        lon_out[0, t] = horizontal_ref[0, :, CLON - 1, :] * mixed_ref[:, CLON - 1, :]
         edge_copy(t, 0).start()
+        lon_out[1, t] = horizontal_ref[1, :, 0, :] * mixed_ref[:, 0, :]
         edge_copy(t, 1).start()
-        lat_out[0, t] = jnp.sum(jnp.where(
-            lane == level, jnp.broadcast_to(north[:, :, CLAT - 1:CLAT], shape), 0.0), axis=0)
-        lat_out[1, t] = jnp.sum(jnp.where(
-            lane == level, jnp.broadcast_to(south[:, :, 0:1], shape), 0.0), axis=0)
+        for side in range(2):
+            for g in range(groups):
+                lat_out[side, t, g] = edge_ref[side, g] * edges[side][g]
 
         @pl.when(lat < lats - 1)
         def _():
@@ -301,12 +333,20 @@
         def _():
             edge_copy(t, 3).start()
 
-        inside = (diagonal_ref[...] * mixed
-                  + jnp.where(sub == 0, 0.0, pltpu.roll(term_ref[0], 1, 1))
-                  + jnp.where(sub == CLON - 1, 0.0, pltpu.roll(term_ref[1], CLON - 1, 1))
-                  + jnp.where(lane == 0, 0.0, pltpu.roll(north, 1, 2))
-                  + jnp.where(lane == CLAT - 1, 0.0, pltpu.roll(south, CLAT - 1, 2)))
-        adjoint_ref[...] = inside
+        for a in chunks:
+            here = slice(a, a + 8)
+            mixed = mixed_ref[here]
+            adjoint_ref[here] = (diagonal_ref[here] * mixed
+                                 + weight_ref[0, here] * pltpu.roll(mixed, 1, 1)
+                                 + weight_ref[1, here] * pltpu.roll(mixed, CLON - 1, 1)
+                                 + weight_ref[2, here] * pltpu.roll(mixed, 1, 2)
+                                 + weight_ref[3, here] * pltpu.roll(mixed, CLAT - 1, 2))
+
+        j = jnp.maximum(STEPS - 2 - t, 0)
+
+        @pl.when(t < STEPS - 1)
+        def _():
+            orbit_copy(j).wait_recv()
 
         @pl.when(lat > 0)
         def _():
@@ -318,15 +358,19 @@
 
         edge_copy(t, 0).wait_recv()
         edge_copy(t, 1).wait_recv()
-        low = jnp.sum(jnp.where(lane == level, lat_in[0, t][None], 0.0), axis=2, keepdims=True)
-        high = jnp.sum(jnp.where(lane == level, lat_in[1, t][None], 0.0), axis=2, keepdims=True)
-        first = lon_in[0, t].reshape(levels, 1, CLAT)
-        last = lon_in[1, t].reshape(levels, 1, CLAT)
-        result = (adjoint_ref[...]
-                  + jnp.where(sub == 0, first, 0.0) + jnp.where(sub == CLON - 1, last, 0.0)
-                  + jnp.where(lane == 0, low, 0.0) + jnp.where(lane == CLAT - 1, high, 0.0))
-        adjoint_ref[...] = result
-        flux_ref[...] += result[0]
+        adjoint_ref[:, 0, :] = adjoint_ref[:, 0, :] + lon_in[0, t]
+        adjoint_ref[:, CLON - 1, :] = adjoint_ref[:, CLON - 1, :] + lon_in[1, t]
+        bins = bins_ref[j] + other_ref[j]
+        sides = [lat_in[0, t, g] + lat_in[1, t, g] for g in range(groups)]
+        outer = (lane == 0) | (lane == CLAT - 1)
+        for a in chunks:
+            near = jnp.stack([pltpu.roll(sides[l // pairs], -2 * l % CLAT, 1)
+                              for l in range(a, a + 8)])
+            result = adjoint_ref[a:a + 8] + jnp.where(outer, near, 0.0)
+            adjoint_ref[a:a + 8] = result
+            forced_ref[a:a + 8] = result + force(bins, a)
+            if a == 0:
+                flux_ref[...] += result[0]
         return 0
 
     lax.fori_loop(0, STEPS, advance, 0)
@@ -355,6 +399,7 @@
     orbits, lons, lats = (lax.axis_size(name) for name in ("orbit", "lon", "lat"))
     vmem = pl.BlockSpec(memory_space=pltpu.VMEM)
     block = (levels, CLON, CLAT)
+    groups = -(-2 * levels // CLAT)
     return pl.pallas_call(
         functools.partial(steps_kernel, orbits, lons, lats, level_weights(levels, kernel_levels)),
         out_shape=(jax.ShapeDtypeStruct(block, F32), jax.ShapeDtypeStruct((CLON, CLAT), F32)),
@@ -362,12 +407,15 @@
         out_specs=(vmem, vmem),
         scratch_shapes=[
             pltpu.VMEM(bins.shape, F32),
-            pltpu.VMEM((2,) + block, F32),
             pltpu.VMEM(block, F32),
+            pltpu.VMEM(block, F32),
+            pltpu.VMEM(block, F32),
+            pltpu.VMEM((4,) + block, F32),
+            pltpu.VMEM((2, groups, CLON, CLAT), F32),
             pltpu.VMEM((2, STEPS, levels, CLAT), F32),
             pltpu.VMEM((2, STEPS, levels, CLAT), F32),
-            pltpu.VMEM((2, STEPS, CLON, CLAT), F32),
-            pltpu.VMEM((2, STEPS, CLON, CLAT), F32),
+            pltpu.VMEM((2, STEPS, groups, CLON, CLAT), F32),
+            pltpu.VMEM((2, STEPS, groups, CLON, CLAT), F32),
             pltpu.SemaphoreType.DMA((STEPS,)),
             pltpu.SemaphoreType.DMA((STEPS,)),
             pltpu.SemaphoreType.DMA((4, STEPS)),

time: 113 us -> 112 us (level)
  no operation moved by 1% of the time
where the time goes in v3:
time: 112 us; the launch traced here: 111 us
  Pallas kernels  105 us (94%)
  local copies, waits for them, and re-layouts  3.75 us (3%)
  other arithmetic  1.62 us (1%)
    pallas_call x1, Pallas kernels, transport(): pl.pallas_call(functools.partial(steps_kernel, orbits, lons, lats, level_...  51.1 us
    pallas_call x1, Pallas kernels, bin_soundings(): pl.pallas_call(functools.partial(bin_kernel, levels, lons, lats), out_sha...  38.8 us
    pallas_call x1, Pallas kernels, pack(): pl.pallas_call(functools.partial(pack_kernel, owners, capacity), out_shap...  15.2 us
    unnamed x12, local copies, waits for them, and re-layouts  3.75 us

profile of v3, /device:TPU:0, one launch (start us, length us, event | category | flops | bytes accessed | tf_op | source)
XLA Modules:
  0.0 111.3 jit_solution(5331725551997748109)
XLA Ops:
  0.6 0.9 convert_reduce_fusion.starts_ref
  1.5 0.7 multiply_add_fusion
  2.2 0.0 copy-start.1
  2.2 1.0 copy-done.1
  3.2 0.0 copy-start.3
  3.2 0.7 copy-done.3
  4.0 0.0 copy-start.4
  4.0 0.7 copy-done.4
  4.7 15.2 %shard_map.86.slots_ref = f32[16,21,1024]{2,1,0:T(8,128)S(1)} custom-call(s32[17]{0:T(128)S(1)} %convert_reduce_fusion.starts_ref, f32[20,4096]{1,0:T(8,128)S(1)} %copy-done.1, f32[1,4096]{1,0:T(1,128)S(1)} %bitcast.7, s32[1,4096]{1,0:T(1,128)S(1)} %bitcast.6, s32[1,4096]{1,0:T(1,128)S(1)} %bitcast.4), custom_call_target="tpu_custom_call" | custom-call | tf_op jit(solution)/shard_map/pallas_call | solution.py:103
  19.9 0.0 copy-start
  19.9 0.0 copy-start.2
  19.9 38.8 %shard_map.87.bins_ref = f32[8,20,8,128]{3,2,1,0:T(8,128)S(1)} custom-call(f32[16,21,1024]{2,1,0:T(8,128)S(1)} %shard_map.86.slots_ref), custom_call_target="tpu_custom_call" | custom-call | tf_op jit(solution)/shard_map/pallas_call | solution.py:192
  58.8 0.0 copy-done
  58.8 0.0 copy-done.2
  58.8 51.1 %shard_map.88 = (f32[72,8,128]{2,1,0:T(8,128)S(1)}, f32[8,128]{1,0:T(8,128)S(1)}) custom-call(f32[8,20,8,128]{3,2,1,0:T(8,128)S(1)} %shard_map.87.bins_ref, f32[4,72,8,128]{3,2,1,0:T(8,128)S(1)} %copy-done, f32[71,8,128]{2,1,0:T(8,128)S(1)} %copy-done.2), custom_call_target="tpu_custom_call" | custom-call | tf_op jit(solution)/shard_map/pallas_call | solution.py:403
  109.9 0.7 copy.11
  110.7 0.6 copy.12
Async XLA Ops:
  2.2 1.0 copy-start.1
  3.2 0.7 copy-start.3
  4.0 0.7 copy-start.4
  19.9 38.9 %copy-start = (f32[4,72,8,128]{3,2,1,0:T(8,128)S(1)}, f32[4,72,8,128]{3,2,1,0:T(8,128)}, u32[]{:S(2)}) copy-start(f32[4,72,8,128]{3,2,1,0:T(8,128)} %horizontal_ref.1) | copy-start | bytes 3538948
  19.9 38.9 %copy-start.2 = (f32[71,8,128]{2,1,0:T(8,128)S(1)}, f32[71,8,128]{2,1,0:T(8,128)}, u32[]{:S(2)}) copy-start(f32[71,8,128]{2,1,0:T(8,128)} %vertical_ref.1) | copy-start | bytes 872452

commit v4 on v3

--- a/solution.py
+++ b/solution.py
@@ -14,6 +14,7 @@
 CELLS = CLON * CLAT
 ROWS = 24
 CHUNK = 256
+AHEAD = 2
 F32 = jnp.float32
 BF16 = jnp.bfloat16
 VMEM_LIMIT = 48 * 1024 * 1024
@@ -248,7 +249,7 @@
         orbit_copy(STEPS - 1 - t).start()
         return 0
 
-    lax.fori_loop(0, STEPS, begin, 0)
+    lax.fori_loop(0, AHEAD, begin, 0)
 
     @pl.when(lat == 0)
     def _():
@@ -332,6 +333,10 @@
         @pl.when(lat > 0)
         def _():
             edge_copy(t, 3).start()
+
+        @pl.when(t < STEPS - AHEAD)
+        def _():
+            orbit_copy(jnp.maximum(STEPS - 1 - AHEAD - t, 0)).start()
 
         for a in chunks:
             here = slice(a, a + 8)

time: 112 us -> 112 us (level)
  no operation moved by 1% of the time
where the time goes in v4:
time: 112 us; the launch traced here: 111 us
  Pallas kernels  105 us (94%)
  local copies, waits for them, and re-layouts  3.75 us (3%)
  other arithmetic  1.62 us (1%)
    pallas_call x1, Pallas kernels, transport(): pl.pallas_call(functools.partial(steps_kernel, orbits, lons, lats, level_...  51.1 us
    pallas_call x1, Pallas kernels, bin_soundings(): pl.pallas_call(functools.partial(bin_kernel, levels, lons, lats), out_sha...  38.8 us
    pallas_call x1, Pallas kernels, pack(): pl.pallas_call(functools.partial(pack_kernel, owners, capacity), out_shap...  15.2 us
    unnamed x12, local copies, waits for them, and re-layouts  3.75 us

profile of v4, /device:TPU:0, one launch (start us, length us, event | category | flops | bytes accessed | tf_op | source)
XLA Modules:
  0.0 111.2 jit_solution(18244493777953574327)
XLA Ops:
  0.6 0.9 convert_reduce_fusion.starts_ref
  1.5 0.7 multiply_add_fusion
  2.2 0.0 copy-start.1
  2.2 1.0 copy-done.1
  3.2 0.0 copy-start.3
  3.2 0.7 copy-done.3
  4.0 0.0 copy-start.4
  4.0 0.7 copy-done.4
  4.7 15.2 %shard_map.86.slots_ref = f32[16,21,1024]{2,1,0:T(8,128)S(1)} custom-call(s32[17]{0:T(128)S(1)} %convert_reduce_fusion.starts_ref, f32[20,4096]{1,0:T(8,128)S(1)} %copy-done.1, f32[1,4096]{1,0:T(1,128)S(1)} %bitcast.7, s32[1,4096]{1,0:T(1,128)S(1)} %bitcast.6, s32[1,4096]{1,0:T(1,128)S(1)} %bitcast.4), custom_call_target="tpu_custom_call" | custom-call | tf_op jit(solution)/shard_map/pallas_call | solution.py:104
  19.9 0.0 copy-start
  19.9 0.0 copy-start.2
  19.9 38.8 %shard_map.87.bins_ref = f32[8,20,8,128]{3,2,1,0:T(8,128)S(1)} custom-call(f32[16,21,1024]{2,1,0:T(8,128)S(1)} %shard_map.86.slots_ref), custom_call_target="tpu_custom_call" | custom-call | tf_op jit(solution)/shard_map/pallas_call | solution.py:193
  58.8 0.0 copy-done
  58.8 0.0 copy-done.2
  58.8 51.1 %shard_map.88 = (f32[72,8,128]{2,1,0:T(8,128)S(1)}, f32[8,128]{1,0:T(8,128)S(1)}) custom-call(f32[8,20,8,128]{3,2,1,0:T(8,128)S(1)} %shard_map.87.bins_ref, f32[4,72,8,128]{3,2,1,0:T(8,128)S(1)} %copy-done, f32[71,8,128]{2,1,0:T(8,128)S(1)} %copy-done.2), custom_call_target="tpu_custom_call" | custom-call | tf_op jit(solution)/shard_map/pallas_call | solution.py:408
  109.9 0.7 copy.11
  110.7 0.6 copy.12
Async XLA Ops:
  2.2 1.0 copy-start.1
  3.2 0.7 copy-start.3
  4.0 0.7 copy-start.4
  19.9 38.9 %copy-start = (f32[4,72,8,128]{3,2,1,0:T(8,128)S(1)}, f32[4,72,8,128]{3,2,1,0:T(8,128)}, u32[]{:S(2)}) copy-start(f32[4,72,8,128]{3,2,1,0:T(8,128)} %horizontal_ref.1) | copy-start | bytes 3538948
  19.9 38.9 %copy-start.2 = (f32[71,8,128]{2,1,0:T(8,128)S(1)}, f32[71,8,128]{2,1,0:T(8,128)}, u32[]{:S(2)}) copy-start(f32[71,8,128]{2,1,0:T(8,128)} %vertical_ref.1) | copy-start | bytes 872452

commit v5 on v3

--- a/solution.py
+++ b/solution.py
@@ -142,16 +142,21 @@
     lax.fori_loop(1, owners, greet, 0)
     pl.semaphore_wait(barrier, owners - 1)
 
-    def begin(d, _):
-        slot_copy(d).start()
+    def turn(i):
+        return jnp.where(lax.rem(i, 2) == 1, (i + 1) // 2, lax.rem(owners - i // 2, owners))
+
+    def begin(i, _):
+        slot_copy(turn(i)).start()
         return 0
 
     lax.fori_loop(1, owners, begin, 0)
     total_ref[...] = jnp.zeros_like(total_ref)
     got_ref[0] = slots_ref[lon * lats + lat]
 
-    def collect(d, _):
-        @pl.when(d > 0)
+    def collect(i, _):
+        d = turn(i)
+
+        @pl.when(i > 0)
         def _():
             slot_copy(d).wait_recv()
 

time: 112 us -> 109 us (0.973)
  Pallas kernels: 105 us -> 102 us
    pallas_call x1, Pallas kernels: 51.1 us -> 43.2 us  [transport(): pl.pallas_call(functools.partial(steps_kernel, orbits, lons, lats, level_...]
    pallas_call x1, Pallas kernels: 38.8 us -> 43.4 us  [bin_soundings(): pl.pallas_call(functools.partial(bin_kernel, levels, lons, lats), out_sha...]
where the time goes in v5:
time: 109 us; the launch traced here: 108 us
  Pallas kernels  102 us (94%)
  local copies, waits for them, and re-layouts  3.75 us (3%)
  other arithmetic  1.62 us (1%)
    pallas_call x1, Pallas kernels, bin_soundings(): pl.pallas_call(functools.partial(bin_kernel, levels, lons, lats), out_sha...  43.4 us
    pallas_call x1, Pallas kernels, transport(): pl.pallas_call(functools.partial(steps_kernel, orbits, lons, lats, level_...  43.2 us
    pallas_call x1, Pallas kernels, pack(): pl.pallas_call(functools.partial(pack_kernel, owners, capacity), out_shap...  15.2 us
    unnamed x12, local copies, waits for them, and re-layouts  3.75 us

profile of v5, /device:TPU:0, one launch (start us, length us, event | category | flops | bytes accessed | tf_op | source)
XLA Modules:
  0.0 107.9 jit_solution(1424988912987898975)
XLA Ops:
  0.6 0.9 convert_reduce_fusion.starts_ref
  1.5 0.7 multiply_add_fusion
  2.2 0.0 copy-start.1
  2.2 1.0 copy-done.1
  3.2 0.0 copy-start.3
  3.2 0.7 copy-done.3
  4.0 0.0 copy-start.4
  4.0 0.7 copy-done.4
  4.7 15.2 %shard_map.86.slots_ref = f32[16,21,1024]{2,1,0:T(8,128)S(1)} custom-call(s32[17]{0:T(128)S(1)} %convert_reduce_fusion.starts_ref, f32[20,4096]{1,0:T(8,128)S(1)} %copy-done.1, f32[1,4096]{1,0:T(1,128)S(1)} %bitcast.7, s32[1,4096]{1,0:T(1,128)S(1)} %bitcast.6, s32[1,4096]{1,0:T(1,128)S(1)} %bitcast.4), custom_call_target="tpu_custom_call" | custom-call | tf_op jit(solution)/shard_map/pallas_call | solution.py:103
  19.9 0.0 copy-start
  19.9 0.0 copy-start.2
  19.9 43.4 %shard_map.87.bins_ref = f32[8,20,8,128]{3,2,1,0:T(8,128)S(1)} custom-call(f32[16,21,1024]{2,1,0:T(8,128)S(1)} %shard_map.86.slots_ref), custom_call_target="tpu_custom_call" | custom-call | tf_op jit(solution)/shard_map/pallas_call | solution.py:197
  63.3 0.0 copy-done
  63.4 0.0 copy-done.2
  63.4 43.2 %shard_map.88 = (f32[72,8,128]{2,1,0:T(8,128)S(1)}, f32[8,128]{1,0:T(8,128)S(1)}) custom-call(f32[8,20,8,128]{3,2,1,0:T(8,128)S(1)} %shard_map.87.bins_ref, f32[4,72,8,128]{3,2,1,0:T(8,128)S(1)} %copy-done, f32[71,8,128]{2,1,0:T(8,128)S(1)} %copy-done.2), custom_call_target="tpu_custom_call" | custom-call | tf_op jit(solution)/shard_map/pallas_call | solution.py:408
  106.6 0.7 copy.11
  107.3 0.6 copy.12
Async XLA Ops:
  2.2 1.0 copy-start.1
  3.2 0.7 copy-start.3
  4.0 0.7 copy-start.4
  19.9 43.4 %copy-start = (f32[4,72,8,128]{3,2,1,0:T(8,128)S(1)}, f32[4,72,8,128]{3,2,1,0:T(8,128)}, u32[]{:S(2)}) copy-start(f32[4,72,8,128]{3,2,1,0:T(8,128)} %horizontal_ref.1) | copy-start | bytes 3538948
  19.9 43.4 %copy-start.2 = (f32[71,8,128]{2,1,0:T(8,128)S(1)}, f32[71,8,128]{2,1,0:T(8,128)}, u32[]{:S(2)}) copy-start(f32[71,8,128]{2,1,0:T(8,128)} %vertical_ref.1) | copy-start | bytes 872452
